TPU v7x, 128 devices: a whole 4x4x4 slice. The times are simulated.
128 devices in a mesh: tm: 8 (over y_lo, z), space: 16 (over y_hi, x, core).
Axes of the slice: x: 4, y: 4 (y_hi: 2, y_lo: 2; y = y_hi * 2 + y_lo), z: 4, core: 2. Of those that a mesh axis runs over, the one named last changes fastest.
Arguments:
- snapshots: bfloat16 [1024, 786432], P('tm', 'space'), may hold values from -10 to 10, as said below
- area_weight: float32 [786432], P('space'), may hold values from 0.1 to 1
- eigvecs: bfloat16 [1024, 64], replicated, may hold values from -0.1875 to 0.1875
- eigvals: float32 [64], replicated, may hold values from 0.5 to 8
Outputs:
- gram: float32 [1024, 1024], P(('tm', 'space'))
- modes: bfloat16 [64, 786432], P('tm', 'space')
Inputs may be any that keep to these rules, and one draw needn't show every extreme that they name: `snapshots`: a per-column climatology plus hourly departures.
All inputs are finite; a program needn't handle non-finite values.
Results may differ from a plain program's by a relative error of at most 0.01.
Values may be sent and summed in bfloat16 or wider, within the bound.
A program may use at most 128 MiB of HBM per device.

v0:
```python
import jax
import jax.numpy as jnp
from jax import lax
from jax.sharding import PartitionSpec as P


def gram_local(weighted):
    return lax.dot_general(
        weighted, weighted, (((1,), (1,)), ((), ())), preferred_element_type=jnp.float32
    )


def local(snapshots, area_weight, eigvecs, eigvals):
    tm_count = lax.axis_size("tm")
    space_count = lax.axis_size("space")
    time_dev, cell_dev = snapshots.shape
    times = time_dev * tm_count
    cells = cell_dev * space_count
    sub_cells = cell_dev // tm_count
    mode_count = eigvecs.shape[1]
    mode_dev = mode_count // tm_count
    tm_index = lax.axis_index("tm")
    columns = lax.all_to_all(snapshots, "tm", split_axis=1, concat_axis=0, tiled=True)
    mean = jnp.sum(columns.astype(jnp.float32), axis=0) / times
    root = jnp.sqrt(area_weight)
    own_root = lax.dynamic_slice_in_dim(root, tm_index * sub_cells, sub_cells, 0)
    weighted = (own_root[None, :] * (columns.astype(jnp.float32) - mean[None, :])).astype(
        jnp.bfloat16
    )
    partial_gram = gram_local(weighted) / cells
    row_sums = lax.psum_scatter(
        partial_gram.astype(jnp.bfloat16), "tm", scatter_dimension=0, tiled=True
    )
    gram = lax.psum_scatter(row_sums, "space", scatter_dimension=0, tiled=True).astype(jnp.float32)
    inv_root = 1.0 / jnp.sqrt(eigvals)
    all_means = lax.all_gather(mean, "tm", axis=0, tiled=True)
    local_weighted = (root[None, :] * (snapshots.astype(jnp.float32) - all_means[None, :])).astype(
        jnp.bfloat16
    )
    own_rows = lax.dynamic_slice_in_dim(eigvecs, tm_index * time_dev, time_dev, 0)
    summed = lax.psum_scatter(
        jnp.dot(own_rows.T, local_weighted, preferred_element_type=jnp.float32),
        "tm",
        scatter_dimension=0,
        tiled=True,
    )
    own_scale = lax.dynamic_slice_in_dim(inv_root, tm_index * mode_dev, mode_dev, 0)
    modes = (summed * own_scale[:, None]).astype(jnp.bfloat16)
    return (gram, modes)


def solution(mesh):
    in_specs = (P("tm", "space"), P("space"), P(), P())
    out_specs = (P(("tm", "space"), None), P("tm", "space"))
    return jax.shard_map(local, mesh=mesh, in_specs=in_specs, out_specs=out_specs, check_vma=False)
```

profile of v0, /device:TPU:1, one launch (start us, length us, event | category | flops | bytes accessed | tf_op | source)
XLA Modules:
  0.0 477.4 jit_solution(4174322892892114167)
XLA Ops:
  7.2 0.0 copy-start
  7.2 16.5 %copy.8 = bf16[128,49152]{0,1:T(8,128)(2,1)} copy(bf16[128,49152]{1,0:T(8,128)(2,1)} %param.4) | data formatting | bytes 25165824 | tf_op args[0]
  23.7 0.0 copy-start.1
  23.7 7.0 %all-to-all-start = ((bf16[128,8,6144]{0,2,1:T(8,128)(2,1)}), bf16[128,8,6144]{0,2,1:T(8,128)(2,1)}, u32[]{:S(2)}, u32[]{:S(2)}) async-start(bf16[128,8,6144]{0,2,1:T(8,128)(2,1)} %bitcast.6), calls=%async_computation | async-start | bytes 25165824 | tf_op jit(solution)/shard_map/all_to_all | solution.py:23
  30.7 0.0 reduce-scatter.4.cloned.1.call-start
  30.7 0.0 copy-done.1
  30.7 0.1 sqrt.6
  30.8 139.1 %all-to-all-done = bf16[128,8,6144]{0,2,1:T(8,128)(2,1)} async-done(((bf16[128,8,6144]{0,2,1:T(8,128)(2,1)}), bf16[128,8,6144]{0,2,1:T(8,128)(2,1)}, u32[]{:S(2)}, u32[]{:S(2)}) %all-to-all-start) | async-done | bytes 12582944 | tf_op jit(solution)/shard_map/all_to_all | solution.py:23
  169.9 6.3 %convert_reduce_fusion = f32[6144]{0:T(1024)S(1)} fusion(bf16[128,8,6144]{0,2,1:T(8,128)(2,1)} %all-to-all-done), kind=kLoop, calls=%fused_computation.1 | loop fusion | flops 12576768 | bytes 12607488 | tf_op jit(solution)/shard_map/reduce_sum | solution.py:24
  176.2 11.9 %fusion.3 = bf16[8,128,6144]{1,2,0:T(8,128)(2,1)} fusion(bf16[128,8,6144]{0,2,1:T(8,128)(2,1)} %all-to-all-done, f32[6144]{0:T(1024)S(1)} %broadcast_multiply_fusion, f32[6144]{0:T(1024)S(1)} %dynamic_slice.9), kind=kLoop, calls=%fused_computation.6 | loop fusion | flops 25165824 | bytes 25214976 | tf_op jit(solution)/shard_map/convert_element_type | solution.py:27
  188.1 16.7 %copy.9 = bf16[8,128,6144]{2,1,0:T(8,128)(2,1)} copy(bf16[8,128,6144]{1,2,0:T(8,128)(2,1)} %fusion.3) | data formatting | bytes 25165824 | tf_op jit(solution)/shard_map/convert_element_type | solution.py:27
  204.8 19.1 %multiply_convert_fusion.2 = bf16[1024,1024]{1,0:T(8,128)(2,1)} fusion(bf16[1024,6144]{1,0:T(8,128)(2,1)} %bitcast.7), kind=kOutput, calls=%fused_computation.9 | convolution fusion | flops 12886999040 | bytes 14680064 | tf_op jit(solution)/shard_map/dot_general | solution.py:8
  223.8 0.0 reduce-scatter.4.cloned.1.call-update
  223.9 0.0 reduce-scatter.6.cloned.1.call-start
  223.9 23.4 %all_gather.3 = f32[49152]{0:T(1024)S(1)} all-gather(f32[6144]{0:T(1024)S(1)} %broadcast_multiply_fusion), channel_id=1, replica_groups=mesh['tm'=8,'space'=16] {'tm'}, dimensions={0}, use_global_device_ids=true | all-gather | bytes 221184 | tf_op jit(solution)/shard_map/all_gather | solution.py:36
  247.3 14.6 %reduce-scatter.4.cloned.1.call-done = bf16[128,1024]{1,0:T(8,128)(2,1)} async-done(((bf16[1024,1024]{1,0:T(8,128)(2,1)}), bf16[128,1024]{1,0:T(8,128)(2,1)}) %reduce-scatter.4.cloned.1.call-update) | async-done | bytes 262160 | tf_op jit(solution)/shard_map/reduce_scatter | solution.py:31
  261.9 0.0 reduce-scatter.6.cloned.1.call-update
  261.9 0.0 reduce-scatter.8.cloned.1.call-start
  262.0 0.0 copy-done
  262.0 13.2 %fusion.2 = f32[64,49152]{1,0:T(8,128)} fusion(bf16[128,49152]{1,0:T(8,128)(2,1)} %param.4, f32[49152]{0:T(1024)S(1)} %all_gather.3, f32[49152]{0:T(1024)S(1)} %sqrt.6, bf16[1024,64]{0,1:T(8,128)(2,1)S(1)} %copy-done, s32[]{:T(128)S(6)} %select_n.10), kind=kOutput, calls=%fused_computation.5 | convolution fusion | flops 830472192 | bytes 25575428 | tf_op jit(solution)/shard_map/dot_general | solution.py:42
  275.2 0.0 copy-start.2
  275.2 0.0 reduce-scatter.8.cloned.1.call-update
  275.2 0.6 copy-done.2
  275.8 0.1 dynamic_slice.11
  275.9 56.3 %reduce-scatter.6.cloned.1.call-done = bf16[8,1024]{1,0:T(8,128)(2,1)} async-done(((bf16[128,1024]{1,0:T(8,128)(2,1)}), bf16[8,1024]{1,0:T(8,128)(2,1)}) %reduce-scatter.6.cloned.1.call-update) | async-done | bytes 16400 | tf_op jit(solution)/shard_map/reduce_scatter | solution.py:34
  332.2 1.3 convert_element_type.38
  333.6 134.8 %reduce-scatter.8.cloned.1.call-done = f32[8,49152]{1,0:T(8,128)} async-done(((f32[64,49152]{1,0:T(8,128)}), f32[8,49152]{1,0:T(8,128)}) %reduce-scatter.8.cloned.1.call-update) | async-done | bytes 1572880 | tf_op jit(solution)/shard_map/reduce_scatter | solution.py:41
  468.4 2.4 multiply_convert_fusion.3
  (3 shorter events, 0.0 us)
Async XLA Ops:
  7.2 254.8 %copy-start = (bf16[1024,64]{0,1:T(8,128)(2,1)S(1)}, bf16[1024,64]{0,1:T(8,128)(2,1)}, u32[]{:S(2)}) copy-start(bf16[1024,64]{0,1:T(8,128)(2,1)} %param.6) | copy-start | bytes 393220
  23.7 7.1 %copy-start.1 = (f32[49152]{0:T(1024)S(1)}, f32[49152]{0:T(1024)}, u32[]{:S(2)}) copy-start(f32[49152]{0:T(1024)} %param.5) | copy-start | bytes 589828
  23.7 146.3 %all-to-all-start = ((bf16[128,8,6144]{0,2,1:T(8,128)(2,1)}), bf16[128,8,6144]{0,2,1:T(8,128)(2,1)}, u32[]{:S(2)}, u32[]{:S(2)}) async-start(bf16[128,8,6144]{0,2,1:T(8,128)(2,1)} %bitcast.6), calls=%async_computation | async-start | bytes 25165824 | tf_op jit(solution)/shard_map/all_to_all | solution.py:23
  30.7 231.2 %reduce-scatter.4.cloned.1.call-start = ((), (), s32[]{:S(2)}) async-start(), calls=%async_computation.4 | async-start | bytes 2359296 | tf_op jit(solution)/shard_map/reduce_scatter | solution.py:31
  223.9 108.4 %reduce-scatter.6.cloned.1.call-start = ((), (), s32[]{:S(2)}) async-start(), calls=%async_computation.5 | async-start | bytes 278528 | tf_op jit(solution)/shard_map/reduce_scatter | solution.py:34
  261.9 206.5 %reduce-scatter.8.cloned.1.call-start = ((), (), s32[]{:S(2)}) async-start(), calls=%async_computation.6 | async-start | bytes 14155776 | tf_op jit(solution)/shard_map/reduce_scatter | solution.py:41
  275.2 0.7 copy-start.2
Sparse Core Ops, SparseCore 0:
  224.0 37.8 reduce-scatter.3
  265.6 66.5 reduce-scatter.5
  334.8 133.5 reduce-scatter.7
where the time goes:
time: 479 us; the launch traced here: 477 us
  waiting for transfers between devices  345 us (72%)
  local copies, waits for them, and re-layouts  33.9 us (7%)
  matrix products  32.3 us (7%)
  blocking collectives  23.4 us (5%)
  other arithmetic  21.9 us (5%)
  between operations  13.8 us (3%)
  starting transfers between devices  7.12 us (1%)
    all_to_all x1, waiting for transfers between devices, local(): lax.all_to_all(snapshots, 'tm', split_axis=1, concat_axis=0, tiled=True)  139 us
    reduce_scatter x1, waiting for transfers between devices, local(): lax.psum_scatter(jnp.dot(own_rows.T, local_weighted, preferred_element_ty...  135 us
    reduce_scatter x1, waiting for transfers between devices, local(): lax.psum_scatter(row_sums, 'space', scatter_dimension=0, tiled=True)  56.3 us
    all_gather x1, blocking collectives, local(): all_means = lax.all_gather(mean, 'tm', axis=0, tiled=True)  23.4 us
    dot_general x1, matrix products, gram_local(): lax.dot_general(weighted, weighted, (((1,), (1,)), ((), ())), preferred_e...  19.1 us
    unnamed x7, local copies, waits for them, and re-layouts  17.1 us
    convert_element_type x1, local copies, waits for them, and re-layouts, local(): (own_root[None, :] * (columns.astype(jnp.float32) - mean[None, :])).astyp...  16.7 us
    reduce_scatter x1, waiting for transfers between devices, local(): lax.psum_scatter(partial_gram.astype(jnp.bfloat16), 'tm', scatter_dimensi...  14.6 us
  transfers between devices with their start and end apart: 4, of which 4 were waited for; matrix products, arithmetic and copies ran while one was open for 3% of the time, Pallas kernels for 0%

commit v1 on v0

--- a/solution.py
+++ b/solution.py
@@ -20,7 +20,10 @@
     mode_count = eigvecs.shape[1]
     mode_dev = mode_count // tm_count
     tm_index = lax.axis_index("tm")
-    columns = lax.all_to_all(snapshots, "tm", split_axis=1, concat_axis=0, tiled=True)
+    columns = jnp.concatenate(
+        lax.all_to_all(jnp.stack(jnp.split(snapshots, lax.axis_size("tm"), axis=1)), "tm", 0, 0),
+        axis=0,
+    )
     mean = jnp.sum(columns.astype(jnp.float32), axis=0) / times
     root = jnp.sqrt(area_weight)
     own_root = lax.dynamic_slice_in_dim(root, tm_index * sub_cells, sub_cells, 0)

time: 479 us -> 458 us (0.956)
  local copies, waits for them, and re-layouts: 33.9 us -> 22.5 us
    convert_element_type x1 -> x0, local copies, waits for them, and re-layouts: 16.7 us -> none  [local(): (own_root[None, :] * (columns.astype(jnp.float32) - mean[None, :])).astyp...]
    unnamed x7 -> x13, local copies, waits for them, and re-layouts: 17.1 us -> 19.7 us
where the time goes in v1:
time: 458 us; the launch traced here: 457 us
  waiting for transfers between devices  345 us (75%)
  matrix products  27.7 us (6%)
  blocking collectives  23.4 us (5%)
  local copies, waits for them, and re-layouts  22.5 us (5%)
  other arithmetic  17.7 us (4%)
  between operations  13.8 us (3%)
  starting transfers between devices  7.31 us (2%)
    all_to_all x1, waiting for transfers between devices, local(): lax.all_to_all(jnp.stack(jnp.split(snapshots, lax.axis_size('tm'), axis=1...  139 us
    reduce_scatter x1, waiting for transfers between devices, local(): lax.psum_scatter(jnp.dot(own_rows.T, local_weighted, preferred_element_ty...  135 us
    reduce_scatter x1, waiting for transfers between devices, local(): lax.psum_scatter(row_sums, 'space', scatter_dimension=0, tiled=True)  56.3 us
    all_gather x1, blocking collectives, local(): all_means = lax.all_gather(mean, 'tm', axis=0, tiled=True)  23.4 us
    unnamed x13, local copies, waits for them, and re-layouts  19.7 us
    reduce_scatter x1, waiting for transfers between devices, local(): lax.psum_scatter(partial_gram.astype(jnp.bfloat16), 'tm', scatter_dimensi...  14.5 us
    dot_general x1, matrix products, gram_local(): lax.dot_general(weighted, weighted, (((1,), (1,)), ((), ())), preferred_e...  14.4 us
    dot_general x1, matrix products, local(): jnp.dot(own_rows.T, local_weighted, preferred_element_type=jnp.float32)  13.2 us
  transfers between devices with their start and end apart: 4, of which 4 were waited for; matrix products, arithmetic and copies ran while one was open for 3% of the time, Pallas kernels for 0%

profile of v1, /device:TPU:1, one launch (start us, length us, event | category | flops | bytes accessed | tf_op | source)
XLA Modules:
  0.0 457.2 jit_solution(7333703687179740057)
XLA Ops:
  7.2 0.0 copy-start
  7.2 2.8 bitcast_dynamic-update-slice_fusion.7
  10.0 2.7 bitcast_dynamic-update-slice_fusion.6
  12.7 2.7 bitcast_dynamic-update-slice_fusion.5
  15.4 2.7 bitcast_dynamic-update-slice_fusion.4
  18.1 2.7 bitcast_dynamic-update-slice_fusion.3
  20.8 2.7 bitcast_dynamic-update-slice_fusion.2
  23.5 2.8 bitcast_dynamic-update-slice_fusion.1
  26.2 2.7 bitcast_dynamic-update-slice_fusion
  28.9 7.0 %all-to-all-start = ((bf16[8,128,6144]{2,1,0:T(8,128)(2,1)}), bf16[8,128,6144]{2,1,0:T(8,128)(2,1)}, u32[]{:S(2)}, u32[]{:S(2)}) async-start(bf16[8,128,6144]{2,1,0:T(8,128)(2,1)} %bitcast_dynamic-update-slice_fusion), calls=%async_computation | async-start | bytes 25165824 | tf_op jit(solution)/shard_map/all_to_all | solution.py:24
  36.0 0.0 reduce-scatter.4.cloned.1.call-start
  36.0 0.0 copy-done.1
  36.0 0.1 sqrt.6
  36.1 139.1 %all-to-all-done = bf16[8,128,6144]{2,1,0:T(8,128)(2,1)} async-done(((bf16[8,128,6144]{2,1,0:T(8,128)(2,1)}), bf16[8,128,6144]{2,1,0:T(8,128)(2,1)}, u32[]{:S(2)}, u32[]{:S(2)}) %all-to-all-start) | async-done | bytes 12582944 | tf_op jit(solution)/shard_map/all_to_all | solution.py:24
  175.2 6.4 %convert_reduce_fusion = f32[6144]{0:T(1024)S(1)} fusion(bf16[8,128,6144]{2,1,0:T(8,128)(2,1)} %all-to-all-done), kind=kLoop, calls=%fused_computation.1 | loop fusion | flops 12576768 | bytes 12607488 | tf_op jit(solution)/shard_map/reduce_sum | solution.py:27
  181.6 7.5 %fusion.1 = bf16[8,128,6144]{2,1,0:T(8,128)(2,1)S(1)} fusion(bf16[8,128,6144]{2,1,0:T(8,128)(2,1)} %all-to-all-done, f32[6144]{0:T(1024)S(1)} %broadcast_multiply_fusion, f32[6144]{0:T(1024)S(1)} %dynamic_slice.9), kind=kLoop, calls=%fused_computation.3 | loop fusion | flops 25165824 | bytes 25214976 | tf_op jit(solution)/shard_map/convert_element_type | solution.py:30
  189.1 14.4 %multiply_convert_fusion.2 = bf16[1024,1024]{1,0:T(8,128)(2,1)} fusion(bf16[1024,6144]{1,0:T(8,128)(2,1)S(1)} %bitcast.19), kind=kOutput, calls=%fused_computation.8 | convolution fusion | flops 12886999040 | bytes 14680064 | tf_op jit(solution)/shard_map/dot_general | solution.py:8
  203.6 0.0 reduce-scatter.4.cloned.1.call-update
  203.6 0.0 reduce-scatter.6.cloned.1.call-start
  203.6 23.4 %all_gather.3 = f32[49152]{0:T(1024)S(1)} all-gather(f32[6144]{0:T(1024)S(1)} %broadcast_multiply_fusion), channel_id=1, replica_groups=mesh['tm'=8,'space'=16] {'tm'}, dimensions={0}, use_global_device_ids=true | all-gather | bytes 221184 | tf_op jit(solution)/shard_map/all_gather | solution.py:39
  227.0 14.5 %reduce-scatter.4.cloned.1.call-done = bf16[128,1024]{1,0:T(8,128)(2,1)} async-done(((bf16[1024,1024]{1,0:T(8,128)(2,1)}), bf16[128,1024]{1,0:T(8,128)(2,1)}) %reduce-scatter.4.cloned.1.call-update) | async-done | bytes 262160 | tf_op jit(solution)/shard_map/reduce_scatter | solution.py:34
  241.6 0.0 reduce-scatter.6.cloned.1.call-update
  241.6 0.2 reduce-scatter.8.cloned.1.call-start
  241.8 0.0 copy-done
  241.8 13.2 %fusion.2 = f32[64,49152]{1,0:T(8,128)} fusion(bf16[128,49152]{1,0:T(8,128)(2,1)} %param.4, f32[49152]{0:T(1024)S(1)} %all_gather.3, f32[49152]{0:T(1024)S(1)} %sqrt.6, bf16[1024,64]{0,1:T(8,128)(2,1)S(1)} %copy-done, s32[]{:T(128)S(6)} %select_n.10), kind=kOutput, calls=%fused_computation.5 | convolution fusion | flops 830472192 | bytes 25575428 | tf_op jit(solution)/shard_map/dot_general | solution.py:45
  255.1 0.0 reduce-scatter.8.cloned.1.call-update
  255.1 0.6 copy-done.2
  255.7 0.1 dynamic_slice.11
  255.8 56.3 %reduce-scatter.6.cloned.1.call-done = bf16[8,1024]{1,0:T(8,128)(2,1)} async-done(((bf16[128,1024]{1,0:T(8,128)(2,1)}), bf16[8,1024]{1,0:T(8,128)(2,1)}) %reduce-scatter.6.cloned.1.call-update) | async-done | bytes 16400 | tf_op jit(solution)/shard_map/reduce_scatter | solution.py:37
  312.1 1.3 convert_element_type.33
  313.5 134.8 %reduce-scatter.8.cloned.1.call-done = f32[8,49152]{1,0:T(8,128)} async-done(((f32[64,49152]{1,0:T(8,128)}), f32[8,49152]{1,0:T(8,128)}) %reduce-scatter.8.cloned.1.call-update) | async-done | bytes 1572880 | tf_op jit(solution)/shard_map/reduce_scatter | solution.py:44
  448.3 2.4 multiply_convert_fusion.3
  (5 shorter events, 0.0 us)
Async XLA Ops:
  7.2 234.7 %copy-start = (bf16[1024,64]{0,1:T(8,128)(2,1)S(1)}, bf16[1024,64]{0,1:T(8,128)(2,1)}, u32[]{:S(2)}) copy-start(bf16[1024,64]{0,1:T(8,128)(2,1)} %param.6) | copy-start | bytes 393220
  28.9 7.1 %copy-start.1 = (f32[49152]{0:T(1024)S(1)}, f32[49152]{0:T(1024)}, u32[]{:S(2)}) copy-start(f32[49152]{0:T(1024)} %param.5) | copy-start | bytes 589828
  28.9 146.3 %all-to-all-start = ((bf16[8,128,6144]{2,1,0:T(8,128)(2,1)}), bf16[8,128,6144]{2,1,0:T(8,128)(2,1)}, u32[]{:S(2)}, u32[]{:S(2)}) async-start(bf16[8,128,6144]{2,1,0:T(8,128)(2,1)} %bitcast_dynamic-update-slice_fusion), calls=%async_computation | async-start | bytes 25165824 | tf_op jit(solution)/shard_map/all_to_all | solution.py:24
  36.0 205.6 %reduce-scatter.4.cloned.1.call-start = ((), (), s32[]{:S(2)}) async-start(), calls=%async_computation.4 | async-start | bytes 2359296 | tf_op jit(solution)/shard_map/reduce_scatter | solution.py:34
  203.6 108.6 %reduce-scatter.6.cloned.1.call-start = ((), (), s32[]{:S(2)}) async-start(), calls=%async_computation.5 | async-start | bytes 278528 | tf_op jit(solution)/shard_map/reduce_scatter | solution.py:37
  241.6 206.7 %reduce-scatter.8.cloned.1.call-start = ((), (), s32[]{:S(2)}) async-start(), calls=%async_computation.6 | async-start | bytes 14155776 | tf_op jit(solution)/shard_map/reduce_scatter | solution.py:44
  255.1 0.7 copy-start.2
Sparse Core Ops, SparseCore 0:
  203.7 37.8 reduce-scatter.3
  245.3 66.7 reduce-scatter.5
  314.7 133.5 reduce-scatter.7
